TPU v7x, 256 devices: a whole 4x4x8 slice. The times are simulated.
256 devices in a mesh: dp: 64 (over y, z, core), tensor: 4 (over x).
Axes of the slice: x: 4, y: 4, z: 8, core: 2. Of those that a mesh axis runs over, the one named last changes fastest.
Arguments:
- tokens: bfloat16 [32768, 2560], P('dp', 'tensor'), as said below
- grad_out: bfloat16 [32768, 7168], P('dp', 'tensor'), may hold values from -6 to 6
- error: bfloat16 [64, 2560, 7168], P('dp', None, 'tensor'), may hold values from -120 to 120
- q_start: bfloat16 [7168, 32], P('tensor'), may hold values from -6 to 6
Outputs:
- p_factor: float32 [2560, 32], replicated
- q_factor: float32 [7168, 32], P('tensor')
Inputs may be any that keep to these rules, and one draw needn't show every extreme that they name: `tokens`: activations.
All inputs are finite; a program needn't handle non-finite values.
Results may differ from a plain program's by a relative error of at most 0.014.
Values may be sent and summed in bfloat16 or wider, within the bound.
A program may use at most 128 MiB of HBM per device.

v0:
```python
import math

import jax
import jax.numpy as jnp
from jax import lax
from jax.sharding import PartitionSpec as P


def orthonormal(p_sum, width):
    gram = jnp.dot(p_sum.T, p_sum, precision=lax.Precision.HIGHEST)
    lower = jnp.linalg.cholesky(gram)
    return lax.linalg.triangular_solve(
        lower, p_sum, left_side=False, lower=True, transpose_a=True
    ) * math.sqrt(width)


def on_device(tokens, grad_out, error, q_start):
    memory = error[0]
    width = memory.shape[0]
    q_wide = q_start.astype(jnp.float32)
    grad = lax.dot_general(
        lax.all_gather(tokens, "tensor", axis=1, tiled=True),
        grad_out,
        (((0,), (0,)), ((), ())),
        preferred_element_type=jnp.float32,
    )
    merged = grad + memory.astype(jnp.float32)
    local_p = jnp.dot(merged, q_wide, precision=lax.Precision.HIGHEST)
    p_sum = lax.psum(local_p, ("dp", "tensor"))
    p_factor = orthonormal(p_sum, width)
    p_half = p_factor.astype(jnp.bfloat16)
    p_wide = p_half.astype(jnp.float32)
    local_q = lax.dot_general(
        merged, p_wide, (((0,), (0,)), ((), ())), precision=lax.Precision.HIGHEST
    )
    q_total = lax.psum(local_q, "dp")
    q_factor = q_total / (lax.axis_size("dp") * width)
    return (p_factor, q_factor)


def solution(mesh):
    in_specs = (P("dp", "tensor"), P("dp", "tensor"), P("dp", None, "tensor"), P("tensor", None))
    out_specs = (P(), P("tensor", None))
    return jax.shard_map(
        on_device, mesh=mesh, in_specs=in_specs, out_specs=out_specs, check_vma=False
    )
```

profile of v0, /device:TPU:1, one launch (start us, length us, event | category | flops | bytes accessed | tf_op | source)
XLA Modules:
  0.0 527.2 jit_solution(17090862328544291713)
XLA Ops:
  7.2 0.0 copy-start
  7.2 0.0 all-gather.2.cloned.1.call-start
  7.2 0.7 all-gather.2.cloned.1.call-update
  7.9 0.0 copy-start.2
  7.9 0.0 all-reduce.3.cloned.1.call-start
  8.0 43.4 %all-gather.2.cloned.1.call-done = bf16[512,2560]{1,0:T(8,128)(2,1)} async-done(((bf16[512,640]{1,0:T(8,128)(2,1)}), bf16[512,2560]{1,0:T(8,128)(2,1)}) %all-gather.2.cloned.1.call-update) | async-done | bytes 2621456 | tf_op jit(solution)/shard_map/all_gather | solution.py:22
  51.4 0.0 copy-done
  51.4 11.2 %fusion.8 = f32[2560,1792]{1,0:T(8,128)} fusion(bf16[512,2560]{1,0:T(8,128)(2,1)} %all-gather.2.cloned.1.call-done, bf16[512,1792]{1,0:T(8,128)(2,1)S(1)} %copy-done), kind=kOutput, calls=%fused_computation.17 | convolution fusion | flops 4697620480 | bytes 22806528 | tf_op jit(solution)/shard_map/dot_general | solution.py:21
  62.6 0.0 copy-done.2
  62.6 16.1 %fusion.1 = f32[2560,32]{0,1:T(8,128)} fusion(bf16[1792,32]{0,1:T(8,128)(2,1)S(1)} %copy-done.2, f32[2560,1792]{1,0:T(8,128)} %fusion.8, bf16[1,2560,1792]{2,1,0:T(8,128)(2,1)} %param.6), kind=kOutput, calls=%fused_computation.2 | convolution fusion | flops 1770782720 | bytes 27967488 | tf_op jit(solution)/shard_map/dot_general | solution.py:28
  78.6 0.0 all-reduce.3.cloned.1.call-update
  78.7 0.2 all-reduce.5.cloned.1.call-start
  78.9 246.0 %all-reduce.3.cloned.1.call-done = f32[2560,32]{0,1:T(8,128)} async-done(((f32[2560,32]{0,1:T(8,128)}), f32[2560,32]{0,1:T(8,128)}) %all-reduce.3.cloned.1.call-update) | async-done | bytes 327696 | tf_op jit(solution)/shard_map/psum | solution.py:29
  324.9 1.5 fusion.9
  326.3 0.1 copy.6
  326.4 2.9 cholesky.16
  329.4 0.6 compare_reduce_fusion
  330.0 0.7 fusion.5
  330.7 2.4 custom-call.6
  333.1 1.4 convolution_multiply_fusion
  334.6 0.0 copy-start.1
  334.6 13.3 %fusion = f32[1792,32]{0,1:T(8,128)} fusion(f32[2560,1792]{1,0:T(8,128)} %fusion.8, bf16[1,2560,1792]{2,1,0:T(8,128)(2,1)} %param.6, f32[2560,32]{0,1:T(8,128)S(1)} %convolution_multiply_fusion), kind=kOutput, calls=%fused_computation.1 | convolution fusion | flops 1770864640 | bytes 28082176 | tf_op jit(solution)/shard_map/dot_general | solution.py:33
  347.9 0.0 copy-done.1
  347.9 0.0 all-reduce.5.cloned.1.call-update
  347.9 171.1 %all-reduce.5.cloned.1.call-done = f32[1792,32]{0,1:T(8,128)} async-done(((f32[1792,32]{0,1:T(8,128)}), f32[1792,32]{0,1:T(8,128)}) %all-reduce.5.cloned.1.call-update) | async-done | bytes 229392 | tf_op jit(solution)/shard_map/psum | solution.py:36
  519.1 1.6 broadcast_multiply_fusion
  (2 shorter events, 0.0 us)
Async XLA Ops:
  7.2 44.2 %copy-start = (bf16[512,1792]{1,0:T(8,128)(2,1)S(1)}, bf16[512,1792]{1,0:T(8,128)(2,1)}, u32[]{:S(2)}) copy-start(bf16[512,1792]{1,0:T(8,128)(2,1)} %param.5) | copy-start | bytes 5505028
  7.2 44.2 %all-gather.2.cloned.1.call-start = ((), (), s32[]{:S(2)}) async-start(), calls=%async_computation | async-start | bytes 3276800 | tf_op jit(solution)/shard_map/all_gather | solution.py:22
  7.9 54.6 %copy-start.2 = (bf16[1792,32]{0,1:T(8,128)(2,1)S(1)}, bf16[1792,32]{0,1:T(8,128)(2,1)}, u32[]{:S(2)}) copy-start(bf16[1792,32]{0,1:T(8,128)(2,1)} %param.7) | copy-start | bytes 344068
  7.9 316.9 %all-reduce.3.cloned.1.call-start = ((), (), s32[]{:S(2)}) async-start(), calls=%async_computation.1 | async-start | bytes 655360 | tf_op jit(solution)/shard_map/psum | solution.py:29
  78.7 440.4 %all-reduce.5.cloned.1.call-start = ((), (), s32[]{:S(2)}) async-start(), calls=%async_computation.2 | async-start | bytes 458752 | tf_op jit(solution)/shard_map/psum | solution.py:36
  334.6 13.3 %copy-start.1 = (f32[2560,32]{0,1:T(8,128)}, f32[2560,32]{0,1:T(8,128)S(1)}, u32[]{:S(2)}) copy-start(f32[2560,32]{0,1:T(8,128)S(1)} %convolution_multiply_fusion) | copy-start | bytes 983044
Sparse Core Ops, SparseCore 0:
  9.8 41.5 all-gather.1
  78.8 246.0 all-reduce.2
  348.1 170.9 all-reduce.4
where the time goes:
time: 527 us
  waiting for transfers between devices  461 us (87%)
  matrix products  43.5 us (8%)
  between operations  13.8 us (3%)
  other arithmetic  8.34 us (2%)
    psum x1, waiting for transfers between devices, on_device(): p_sum = lax.psum(local_p, ('dp', 'tensor'))  246 us
    psum x1, waiting for transfers between devices, on_device(): q_total = lax.psum(local_q, 'dp')  171 us
    all_gather x1, waiting for transfers between devices, on_device(): lax.all_gather(tokens, 'tensor', axis=1, tiled=True)  43.4 us
    dot_general x1, matrix products, on_device(): local_p = jnp.dot(merged, q_wide, precision=lax.Precision.HIGHEST)  16.1 us
    dot_general x1, matrix products, on_device(): lax.dot_general(merged, p_wide, (((0,), (0,)), ((), ())), precision=lax.P...  13.3 us
    dot_general x1, matrix products, on_device(): lax.dot_general(lax.all_gather(tokens, 'tensor', axis=1, tiled=True), gra...  11.2 us
  transfers between devices with their start and end apart: 3, of which 3 were waited for; matrix products, arithmetic and copies ran while one was open for 0% of the time, Pallas kernels for 0%

commit v1 on v0

v1 whole, which is shorter than its diff:
```python
import functools
import math

import jax
import jax.numpy as jnp
from jax import lax
from jax.experimental import pallas as pl
from jax.experimental.pallas import tpu as pltpu
from jax.sharding import PartitionSpec as P

MESH = pl.DeviceIdType.MESH
NX, NY, NZ, NC = 4, 4, 8, 2
CHUNKS = 5
BF16, F32 = jnp.bfloat16, jnp.float32
NN = (((1,), (0,)), ((), ()))
NT = (((1,), (1,)), ((), ()))


def mm(a, b, dims, precision=None):
    return lax.dot_general(a, b, dims, precision=precision, preferred_element_type=F32)


def two_part(value):
    high = value.astype(BF16)
    low = (value - high.astype(F32)).astype(BF16)
    return jnp.concatenate([high, low], axis=0)


def folded(value):
    half = value.shape[0] // 2
    return value[:half] + value[half:]


def inverse_factor(gram):
    n = gram.shape[0]
    rows = lax.broadcasted_iota(jnp.int32, (n, n), 0)
    columns = lax.broadcasted_iota(jnp.int32, (n, n), 1)
    unit = (rows == columns).astype(F32)
    both = jnp.concatenate([gram, unit], axis=1)
    at_row = lax.broadcasted_iota(jnp.int32, (n, 1), 0)
    for j in range(n):
        pivot = both[j : j + 1, :]
        scale = both[:, j : j + 1] / pivot[:, j : j + 1]
        both = both - jnp.where(at_row > j, scale, 0.0) * pivot
    diagonal = jnp.sum(jnp.where(rows == columns, both[:, :n], 0.0), axis=1, keepdims=True)
    return both[:, n:] / jnp.sqrt(diagonal)


def kernel(
    tokens_hbm, outs_hbm, error_hbm, q_hbm, p_ref, q_ref,
    tokens, outs, error, q, gq, gq_in, p_mine, p_core, p_xy, p_z, p_all, p_part,
    v, v_in, u, u_core, u_y, u_z, u_all,
    load_sem, gq_sem, core_sem, xy_sem, z_sem, all_sem, sib_sem, v_sem, ucore_sem, uy_sem, uz_sem, uall_sem, usib_sem,
):
    dp, x = lax.axis_index("dp"), lax.axis_index("tensor")
    core, z, y = dp % NC, (dp // NC) % NZ, dp // (NC * NZ)
    width, rank = error.shape[0], q.shape[0]
    half, own_width = rank // 2, tokens.shape[1]
    rows = width // CHUNKS

    def device(dx=0, dy=0, dz=0, dc=0):
        there = ((y + dy) % NY * NZ + (z + dz) % NZ) * NC + (core + dc) % NC
        return (there, (x + dx) % NX)

    sends = []

    def push(src, dst, sems, index, where):
        copy = pltpu.make_async_remote_copy(
            src_ref=src, dst_ref=dst, send_sem=sems.at[0, index], recv_sem=sems.at[1, index],
            device_id=where, device_id_type=MESH,
        )
        copy.start()
        sends.append(copy)
        return copy

    loads = [
        pltpu.make_async_copy(q_hbm, q, load_sem.at[0]),
        pltpu.make_async_copy(outs_hbm, outs, load_sem.at[1]),
    ]
    for k in range(CHUNKS):
        part = pl.ds(k * rows, rows)
        loads.append(pltpu.make_async_copy(error_hbm.at[part], error.at[part], load_sem.at[3 + k]))
    loads.append(pltpu.make_async_copy(tokens_hbm, tokens, load_sem.at[2]))
    for load in loads:
        load.start()

    plane = [(dx, dy) for dx in range(NX) for dy in range(NY) if dx or dy]
    barrier = pltpu.get_barrier_semaphore()
    friends = [device(dx, dy) for dx, dy in plane]
    friends += [device(dz=d) for d in range(1, NZ)] + [device(dc=1)]
    for friend in friends:
        pl.semaphore_signal(barrier, inc=1, device_id=friend, device_id_type=MESH)

    loads[0].wait()
    loads[1].wait()
    gq[...] = mm(q[...], outs[...], NT)
    pl.semaphore_wait(barrier, len(friends))
    gq_copies = [push(gq, gq_in.at[d - 1], gq_sem, d - 1, device(dx=d)) for d in range(1, NX)]

    for k in range(CHUNKS):
        loads[2 + k].wait()
        p_mine[:, k * rows : (k + 1) * rows] = mm(q[...], error[k * rows : (k + 1) * rows, :], NT)

    loads[2 + CHUNKS].wait()
    for copy in gq_copies:
        copy.wait_recv()
    total = gq[...] + gq_in[0] + gq_in[1] + gq_in[2]
    own = pl.ds(pl.multiple_of(x * own_width, 128), own_width)
    p_mine[:, own] = p_mine[:, own] + folded(mm(two_part(total), tokens[...], NN))

    mine, other = pl.ds(core * half, half), pl.ds((1 - core) * half, half)
    push(p_mine.at[other], p_core, core_sem, 0, device(dc=1)).wait_recv()
    p_core[...] = p_core[...] + p_mine[mine, :]

    def piece(dx, dy):
        to = (x + dx) % NX * NY + (y + dy) % NY
        at = pl.multiple_of(5 * (to % 8) // 2 * 128, 128)
        return p_core.at[pl.ds(pl.multiple_of(to // 8 * 8, 8), 8), pl.ds(at, 384)]

    copies = [push(piece(*d), p_xy.at[i], xy_sem, i, device(*d)) for i, d in enumerate(plane)]
    total = piece(0, 0)[...]
    for i, copy in enumerate(copies):
        copy.wait_recv()
        total = total + p_xy[i]

    p_z[z] = total
    copies = [push(p_z.at[z], p_z.at[z], z_sem, d - 1, device(dz=d)) for d in range(1, NZ)]
    for copy in copies:
        copy.wait_recv()
    total = p_z[0]
    for d in range(1, NZ):
        total = total + p_z[d]

    me = x * NY + y
    slot = p_all.at[core, me]
    slot[...] = total
    copies = [push(slot, slot, all_sem, i, device(*d)) for i, d in enumerate(plane)]
    for copy in copies:
        copy.wait_recv()
    push(p_all.at[core], p_all.at[core], sib_sem, 0, device(dc=1)).wait_recv()
    for c in range(NC):
        for r in range(2):
            rank_rows = slice(16 * c + 8 * r, 16 * c + 8 * r + 8)
            for g in range(4):
                p_mine_at = 640 * g
                p_ref[rank_rows, p_mine_at : p_mine_at + 384] = p_all[c, 8 * r + 2 * g]
                p_ref[rank_rows, p_mine_at + 384 : p_mine_at + 640] = p_all[c, 8 * r + 2 * g + 1, :, 128:384]

    p_part[...] = two_part(p_ref[...])
    v[...] = folded(mm(p_part[:, own], tokens[...], NT))
    v_copies = [push(v, v_in.at[d - 1], v_sem, d - 1, device(dx=d)) for d in range(1, NX)]
    from_error = folded(mm(p_part[...], error[...], NN))
    for copy in v_copies:
        copy.wait_recv()
    total = two_part(v[...] + v_in[0] + v_in[1] + v_in[2])
    u[...] = from_error + folded(mm(total, outs[...], NN))

    push(u.at[other], u_core, ucore_sem, 0, device(dc=1)).wait_recv()
    u_core[...] = u_core[...] + u[mine, :]
    long = u_core.shape[1] // 2

    def quarter(dy):
        to = (y + dy) % NY
        at = pl.multiple_of(to % 2 * long, 128)
        return u_core.at[pl.ds(pl.multiple_of(to // 2 * 8, 8), 8), pl.ds(at, long)]

    copies = [push(quarter(d), u_y.at[d - 1], uy_sem, d - 1, device(dy=d)) for d in range(1, NY)]
    total = quarter(0)[...]
    for i, copy in enumerate(copies):
        copy.wait_recv()
        total = total + u_y[i]
    u_z[z] = total
    copies = [push(u_z.at[z], u_z.at[z], uz_sem, d - 1, device(dz=d)) for d in range(1, NZ)]

    p_sum = p_ref[...]
    gram = mm(p_sum, p_sum, NT, lax.Precision.HIGHEST)
    inverse = inverse_factor(gram)
    p_ref[...] = mm(inverse * math.sqrt(width), p_sum, NN, lax.Precision.HIGHEST)

    for copy in copies:
        copy.wait_recv()
    total = u_z[0]
    for d in range(1, NZ):
        total = total + u_z[d]
    slot = u_all.at[core, y]
    slot[...] = total
    copies = [push(slot, slot, uall_sem, d - 1, device(dy=d)) for d in range(1, NY)]
    for copy in copies:
        copy.wait_recv()
    push(u_all.at[core], u_all.at[core], usib_sem, 0, device(dc=1)).wait_recv()
    scaled = inverse * (1.0 / (NC * NZ * NY * math.sqrt(width)))
    for side in range(2):
        total = jnp.concatenate([u_all[0, side], u_all[0, 2 + side], u_all[1, side], u_all[1, 2 + side]], axis=0)
        q_ref[:, side * long : (side + 1) * long] = mm(scaled, total, NN, lax.Precision.HIGHEST)
    for copy in sends:
        copy.wait_send()


def on_device(tokens, grad_out, error, q_start):
    width, hidden = error.shape[1:]
    rank, count, own_width = q_start.shape[1], tokens.shape[0], tokens.shape[1]
    vmem, dma = pltpu.VMEM, pltpu.SemaphoreType.DMA
    p_factor, q_factor = pl.pallas_call(
        kernel,
        out_shape=(
            jax.ShapeDtypeStruct((rank, width), F32),
            jax.ShapeDtypeStruct((rank, hidden), F32),
        ),
        in_specs=[pl.BlockSpec(memory_space=pl.ANY)] * 4,
        out_specs=(pl.BlockSpec(memory_space=pltpu.VMEM),) * 2,
        scratch_shapes=[
            vmem((count, own_width), BF16),
            vmem((count, hidden), BF16),
            vmem((width, hidden), BF16),
            vmem((rank, hidden), BF16),
            vmem((rank, count), F32),
            vmem((NX - 1, rank, count), F32),
            vmem((rank, width), F32),
            vmem((rank // 2, width), F32),
            vmem((NX * NY - 1, 8, 384), F32),
            vmem((NZ, 8, 384), F32),
            vmem((NC, NX * NY, 8, 384), F32),
            vmem((2 * rank, width), BF16),
            vmem((rank, count), F32),
            vmem((NX - 1, rank, count), F32),
            vmem((rank, hidden), F32),
            vmem((rank // 2, hidden), F32),
            vmem((NY - 1, 8, hidden // 2), F32),
            vmem((NZ, 8, hidden // 2), F32),
            vmem((NC, NY, 8, hidden // 2), F32),
            dma((3 + CHUNKS,)),
            dma((2, NX - 1)),
            dma((2, 1)),
            dma((2, NX * NY - 1)),
            dma((2, NZ - 1)),
            dma((2, NX * NY - 1)),
            dma((2, 1)),
            dma((2, NX - 1)),
            dma((2, 1)),
            dma((2, NY - 1)),
            dma((2, NZ - 1)),
            dma((2, NY - 1)),
            dma((2, 1)),
        ],
        compiler_params=pltpu.CompilerParams(
            collective_id=0, has_side_effects=True, vmem_limit_bytes=44 << 20
        ),
    )(tokens, grad_out, error[0], q_start.T)
    return (p_factor.T, q_factor.T)


def solution(mesh):
    in_specs = (P("dp", "tensor"), P("dp", "tensor"), P("dp", None, "tensor"), P("tensor", None))
    out_specs = (P(), P("tensor", None))
    return jax.shard_map(
        on_device, mesh=mesh, in_specs=in_specs, out_specs=out_specs, check_vma=False
    )
```

time: 527 us -> 65 us (0.12)
  waiting for transfers between devices: 461 us -> 0 us
  Pallas kernels: 0 us -> 59.3 us
  matrix products: 43.5 us -> 0 us
  between operations: 13.8 us -> 0.65 us
  other arithmetic: 8.34 us -> 0 us
    psum x2 -> x0, waiting for transfers between devices: 417 us -> none  [the longest x1 246 us: on_device(): p_sum = lax.psum(local_p, ('dp', 'tensor'))]
    pallas_call x0 -> x1, Pallas kernels: none -> 59.3 us  [on_device(): pl.pallas_call(kernel, out_shape=(jax.ShapeDtypeStruct((rank, width), F32...]
    all_gather x1 -> x0, waiting for transfers between devices: 43.4 us -> none  [on_device(): lax.all_gather(tokens, 'tensor', axis=1, tiled=True)]
    dot_general x4 -> x0, matrix products: 42 us -> none  [the longest x1 16.1 us: on_device(): local_p = jnp.dot(merged, q_wide, precision=lax.Precision.HIGHEST)]
    another operation x5 -> x0, other arithmetic: 6.68 us -> none  [the longest x3 3.6 us: orthonormal(): lower = jnp.linalg.cholesky(gram)]
  transfers between devices with their start and end apart: 3 -> 0, of which waited for: 3 -> 0; matrix products, arithmetic and copies ran while one was open for 0% -> 0% of each run, Pallas kernels for 0% -> 0%
where the time goes in v1:
time: 65 us; the launch traced here: 64.8 us
  Pallas kernels  59.3 us (91%)
  local copies, waits for them, and re-layouts  4.89 us (8%)
  between operations  0.65 us (1%)
    pallas_call x1, Pallas kernels, on_device(): pl.pallas_call(kernel, out_shape=(jax.ShapeDtypeStruct((rank, width), F32...  59.3 us
    unnamed x8, local copies, waits for them, and re-layouts  4.89 us

profile of v1, /device:TPU:1, one launch (start us, length us, event | category | flops | bytes accessed | tf_op | source)
XLA Modules:
  0.0 64.8 jit_solution(17042748834455164810)
XLA Ops:
  0.6 0.0 copy-start
  0.6 1.5 %copy-done = bf16[512,1792]{1,0:T(8,128)(2,1)S(1)} copy-done((bf16[512,1792]{1,0:T(8,128)(2,1)S(1)}, bf16[512,1792]{1,0:T(8,128)(2,1)}, u32[]{:S(2)}) %copy-start) | copy-done | bytes 1835032
  2.1 0.0 copy-start.1
  2.1 1.1 %copy-done.1 = bf16[512,640]{1,0:T(8,128)(2,1)S(1)} copy-done((bf16[512,640]{1,0:T(8,128)(2,1)S(1)}, bf16[512,640]{1,0:T(8,128)(2,1)}, u32[]{:S(2)}) %copy-start.1) | copy-done | bytes 655384
  3.2 0.0 copy-start.2
  3.2 0.9 %copy-done.2 = bf16[1792,32]{0,1:T(8,128)(2,1)S(1)} copy-done((bf16[1792,32]{0,1:T(8,128)(2,1)S(1)}, bf16[1792,32]{0,1:T(8,128)(2,1)}, u32[]{:S(2)}) %copy-start.2) | copy-done | bytes 114712
  4.1 59.3 %shard_map.59 = (f32[32,2560]{1,0:T(8,128)S(1)}, f32[32,1792]{1,0:T(8,128)S(1)}) custom-call(bf16[512,640]{1,0:T(8,128)(2,1)S(1)} %copy-done.1, bf16[512,1792]{1,0:T(8,128)(2,1)S(1)} %copy-done, bf16[2560,1792]{1,0:T(8,128)(2,1)} %bitcast.7, bf16[32,1792]{1,0:T(8,128)(2,1)S(1)} %bitcast.6), custom_call_target="tpu_custom_call" | custom-call | tf_op jit(solution)/shard_map/pallas_call | solution.py:203
  63.4 0.7 %copy.8 = f32[2560,32]{0,1:T(8,128)} copy(f32[2560,32]{0,1:T(8,128)S(1)} %bitcast.4) | data formatting | bytes 655360
  64.1 0.7 %copy.9 = f32[1792,32]{0,1:T(8,128)} copy(f32[1792,32]{0,1:T(8,128)S(1)} %bitcast.5) | data formatting | bytes 458752
Async XLA Ops:
  0.6 1.5 %copy-start = (bf16[512,1792]{1,0:T(8,128)(2,1)S(1)}, bf16[512,1792]{1,0:T(8,128)(2,1)}, u32[]{:S(2)}) copy-start(bf16[512,1792]{1,0:T(8,128)(2,1)} %outs_hbm.1) | copy-start | bytes 5505028
  2.1 1.1 %copy-start.1 = (bf16[512,640]{1,0:T(8,128)(2,1)S(1)}, bf16[512,640]{1,0:T(8,128)(2,1)}, u32[]{:S(2)}) copy-start(bf16[512,640]{1,0:T(8,128)(2,1)} %tokens_hbm.1) | copy-start | bytes 1966084
  3.2 0.9 %copy-start.2 = (bf16[1792,32]{0,1:T(8,128)(2,1)S(1)}, bf16[1792,32]{0,1:T(8,128)(2,1)}, u32[]{:S(2)}) copy-start(bf16[1792,32]{0,1:T(8,128)(2,1)} %param.7) | copy-start | bytes 344068

commit v2 on v1

v2 whole, which is shorter than its diff:
```python
import functools
import math

import jax
import jax.numpy as jnp
from jax import lax
from jax.experimental import pallas as pl
from jax.experimental.pallas import tpu as pltpu
from jax.sharding import PartitionSpec as P

MESH = pl.DeviceIdType.MESH
NX, NY, NZ, NC = 4, 4, 8, 2
FAR_FIRST, NEAR_FIRST = (2, 1, 3), (1, 3, 2)
BF16, F32 = jnp.bfloat16, jnp.float32
NN = (((1,), (0,)), ((), ()))
NT = (((1,), (1,)), ((), ()))


def mm(a, b, dims, precision=None):
    return lax.dot_general(a, b, dims, precision=precision, preferred_element_type=F32)


def two_part(value):
    high = value.astype(BF16)
    low = (value - high.astype(F32)).astype(BF16)
    return jnp.concatenate([high, low], axis=0)


def folded(value):
    half = value.shape[0] // 2
    return value[:half] + value[half:]


def inverse_factor(gram):
    n = gram.shape[0]
    rows = lax.broadcasted_iota(jnp.int32, (n, n), 0)
    columns = lax.broadcasted_iota(jnp.int32, (n, n), 1)
    unit = (rows == columns).astype(F32)
    both = jnp.concatenate([gram, unit], axis=1)
    at_row = lax.broadcasted_iota(jnp.int32, (n, 1), 0)
    for j in range(n):
        pivot = both[j : j + 1, :]
        scale = both[:, j : j + 1] / pivot[:, j : j + 1]
        both = both - jnp.where(at_row > j, scale, 0.0) * pivot
    diagonal = jnp.sum(jnp.where(rows == columns, both[:, :n], 0.0), axis=1, keepdims=True)
    return both[:, n:] / jnp.sqrt(diagonal)


def kernel(
    tokens_hbm, outs_hbm, error_hbm, q_hbm, p_ref, q_ref,
    tokens, outs, error, q, gq, gq_in, p_mine, p_core, p_xy, own, own_in, p_z, p_all,
    v, v_in, u, u_in, u_z, u_all,
    load_sem, gq_sem, core_sem, xy_sem, own_sem, z_sem, near_sem, all_sem, sib_sem, v_sem, u_sem, uz_sem, uall_sem,
):
    dp, x = lax.axis_index("dp"), lax.axis_index("tensor")
    core, z, y = dp % NC, (dp // NC) % NZ, dp // (NC * NZ)
    block, hidden = error.shape[1:]
    width, rank = NX * block, q.shape[0]
    half, long = rank // 2, hidden // 2

    def device(dx=0, dy=0, dz=0, dc=0):
        there = ((y + dy) % NY * NZ + (z + dz) % NZ) * NC + (core + dc) % NC
        return (there, (x + dx) % NX)

    sends = []

    def push(src, dst, sems, index, where):
        copy = pltpu.make_async_remote_copy(
            src_ref=src, dst_ref=dst, send_sem=sems.at[0, index], recv_sem=sems.at[1, index],
            device_id=where, device_id_type=MESH,
        )
        copy.start()
        sends.append(copy)
        return copy

    def load(src, dst, index):
        copy = pltpu.make_async_copy(src, dst, load_sem.at[index])
        copy.start()
        return copy

    q_load = load(q_hbm, q, 0)
    outs_load = load(outs_hbm, outs, 1)
    error_load = {}
    for dx in FAR_FIRST + (0,):
        at = pl.ds(pl.multiple_of((x + dx) % NX * block, block), block)
        error_load[dx] = load(error_hbm.at[at], error.at[dx], 3 + dx)
    tokens_load = load(tokens_hbm, tokens, 2)

    plane = [(dx, dy) for dx in FAR_FIRST for dy in (2, 1, 3, 0)]
    beside = [(dy, dc) for dy in (2, 1, 3, 0) for dc in range(NC) if dy or dc]
    along = (4, 3, 5, 2, 6, 1, 7)
    barrier = pltpu.get_barrier_semaphore()
    friends = [device(dx, dy) for dx, dy in plane] + [device(dy=dy, dc=dc) for dy, dc in beside]
    friends += [device(dz=d) for d in along]
    for friend in friends:
        pl.semaphore_signal(barrier, inc=1, device_id=friend, device_id_type=MESH)

    q_load.wait()
    outs_load.wait()
    gq[...] = mm(q[...], outs[...], NT)
    pl.semaphore_wait(barrier, len(friends))
    gq_copies = [push(gq, gq_in.at[dx - 1], gq_sem, dx - 1, device(dx)) for dx in FAR_FIRST]

    def piece(ref, yy):
        rows = pl.ds(pl.multiple_of(yy // 2 * 8, 8), 8)
        return ref.at[rows, pl.ds(pl.multiple_of(yy % 2 * 256, 128), 384)]

    def pass_on(copy, dx):
        copy.wait_recv()
        p_core[dx - 1] = p_core[dx - 1] + p_mine[dx - 1, core]
        return [
            push(piece(p_core.at[dx - 1], (y + dy) % NY), p_xy.at[4 * (dx - 1) + dy], xy_sem, 4 * (dx - 1) + dy, device(dx, dy))
            for dy in (2, 1, 3, 0)
        ]

    copies, before = [], None
    for dx in FAR_FIRST:
        error_load[dx].wait()
        product = mm(q[...], error[dx], NT)
        p_mine[dx - 1, 0] = product[:half]
        p_mine[dx - 1, 1] = product[half:]
        copy = push(p_mine.at[dx - 1, 1 - core], p_core.at[dx - 1], core_sem, dx - 1, device(dc=1))
        if before is not None:
            copies += pass_on(*before)
        before = (copy, dx)
    error_load[0].wait()
    product = mm(q[...], error[0], NT)
    copies += pass_on(*before)

    tokens_load.wait()
    for copy in gq_copies:
        copy.wait_recv()
    total = gq[...] + gq_in[0] + gq_in[1] + gq_in[2]
    product = product + folded(mm(two_part(total), tokens[...], NN))
    own[0] = product[:half]
    own[1] = product[half:]
    for dy, dc in beside:
        i = 2 * dy + dc - 1
        there = piece(own.at[(core + dc) % NC], (y + dy) % NY)
        copies.append(push(there, own_in.at[i], own_sem, i, device(dy=dy, dc=dc)))
    total = piece(own.at[core], y)[...]
    for copy in copies:
        copy.wait_recv()
    for i in range(12):
        total = total + p_xy[i]
    for i in range(7):
        total = total + own_in[i]

    p_z[z] = total
    copies = [push(p_z.at[z], p_z.at[z], z_sem, d - 1, device(dz=d)) for d in along]
    for copy in copies:
        copy.wait_recv()
    total = p_z[0]
    for d in range(1, NZ):
        total = total + p_z[d]

    slot = p_all.at[x, core, y]
    slot[...] = total
    near = [push(slot, slot, near_sem, 2 * dy + dc - 1, device(dy=dy, dc=dc)) for dy, dc in beside]
    far = {
        dx: [push(slot, slot, all_sem, 4 * (dx - 1) + dy, device(dx, dy)) for dy in (2, 1, 3, 0)]
        for dx in FAR_FIRST
    }

    def features(at):
        rows = []
        for c in range(NC):
            for r in range(2):
                left, right = p_all[at, c, 2 * r], p_all[at, c, 2 * r + 1]
                rows.append(jnp.concatenate([left, right[:, 128:]], axis=1))
        return jnp.concatenate(rows, axis=0)

    for copy in near:
        copy.wait_recv()
    parts = two_part(features(x))
    v[...] = folded(mm(parts, tokens[...], NT))
    v_copies = [push(v, v_in.at[dx - 1], v_sem, dx - 1, device(dx)) for dx in FAR_FIRST]
    result = folded(mm(parts, error[0], NN))
    forward = {}
    for dx in NEAR_FIRST:
        for copy in far[dx]:
            copy.wait_recv()
        rows = p_all.at[(x + NX - dx) % NX, core]
        forward[dx] = push(rows, rows, sib_sem, dx - 1, device(dc=1))
    for dx in NEAR_FIRST:
        forward[dx].wait_recv()
        parts = two_part(features((x + NX - dx) % NX))
        result = result + folded(mm(parts, error[NX - dx], NN))
    for copy in v_copies:
        copy.wait_recv()
    total = two_part(v[...] + v_in[0] + v_in[1] + v_in[2])
    result = result + folded(mm(total, outs[...], NN))

    u[0] = result[:half]
    u[1] = result[half:]

    def quarter(dy, dc):
        to = (y + dy) % NY
        rows = pl.ds(pl.multiple_of(to // 2 * 8, 8), 8)
        return u.at[(core + dc) % NC, rows, pl.ds(pl.multiple_of(to % 2 * long, 128), long)]

    copies = [
        push(quarter(dy, dc), u_in.at[2 * dy + dc - 1], u_sem, 2 * dy + dc - 1, device(dy=dy, dc=dc))
        for dy, dc in beside
    ]
    total = quarter(0, 0)[...]
    for copy in copies:
        copy.wait_recv()
    for i in range(7):
        total = total + u_in[i]
    u_z[z] = total
    copies = [push(u_z.at[z], u_z.at[z], uz_sem, d - 1, device(dz=d)) for d in along]

    for at in range(NX):
        p_ref[:, at * block : (at + 1) * block] = features(at)
    p_sum = p_ref[...]
    gram = mm(p_sum, p_sum, NT, lax.Precision.HIGHEST)
    inverse = inverse_factor(gram)
    p_ref[...] = mm(inverse * math.sqrt(width), p_sum, NN, lax.Precision.HIGHEST)

    for copy in copies:
        copy.wait_recv()
    total = u_z[0]
    for d in range(1, NZ):
        total = total + u_z[d]
    slot = u_all.at[core, y]
    slot[...] = total
    copies = [push(slot, slot, uall_sem, 2 * dy + dc - 1, device(dy=dy, dc=dc)) for dy, dc in beside]
    for copy in copies:
        copy.wait_recv()
    scaled = inverse * (1.0 / (NC * NZ * NY * math.sqrt(width)))
    for side in range(2):
        total = jnp.concatenate([u_all[0, side], u_all[0, 2 + side], u_all[1, side], u_all[1, 2 + side]], axis=0)
        q_ref[:, side * long : (side + 1) * long] = mm(scaled, total, NN, lax.Precision.HIGHEST)
    for copy in sends:
        copy.wait_send()


def on_device(tokens, grad_out, error, q_start):
    width, hidden = error.shape[1:]
    rank, count, own_width = q_start.shape[1], tokens.shape[0], tokens.shape[1]
    vmem, dma = pltpu.VMEM, pltpu.SemaphoreType.DMA
    p_factor, q_factor = pl.pallas_call(
        kernel,
        out_shape=(
            jax.ShapeDtypeStruct((rank, width), F32),
            jax.ShapeDtypeStruct((rank, hidden), F32),
        ),
        in_specs=[pl.BlockSpec(memory_space=pl.ANY)] * 4,
        out_specs=(pl.BlockSpec(memory_space=pltpu.VMEM),) * 2,
        scratch_shapes=[
            vmem((count, own_width), BF16),
            vmem((count, hidden), BF16),
            vmem((NX, own_width, hidden), BF16),
            vmem((rank, hidden), BF16),
            vmem((rank, count), F32),
            vmem((NX - 1, rank, count), F32),
            vmem((NX - 1, NC, rank // 2, own_width), F32),
            vmem((NX - 1, rank // 2, own_width), F32),
            vmem(((NX - 1) * NY, 8, 384), F32),
            vmem((NC, rank // 2, own_width), F32),
            vmem((NC * NY - 1, 8, 384), F32),
            vmem((NZ, 8, 384), F32),
            vmem((NX, NC, NY, 8, 384), F32),
            vmem((rank, count), F32),
            vmem((NX - 1, rank, count), F32),
            vmem((NC, rank // 2, hidden), F32),
            vmem((NC * NY - 1, 8, hidden // 2), F32),
            vmem((NZ, 8, hidden // 2), F32),
            vmem((NC, NY, 8, hidden // 2), F32),
            dma((3 + NX,)),
            dma((2, NX - 1)),
            dma((2, NX - 1)),
            dma((2, (NX - 1) * NY)),
            dma((2, NC * NY - 1)),
            dma((2, NZ - 1)),
            dma((2, NC * NY - 1)),
            dma((2, (NX - 1) * NY)),
            dma((2, NX - 1)),
            dma((2, NX - 1)),
            dma((2, NC * NY - 1)),
            dma((2, NZ - 1)),
            dma((2, NC * NY - 1)),
        ],
        compiler_params=pltpu.CompilerParams(
            collective_id=0, has_side_effects=True, vmem_limit_bytes=60 << 20
        ),
    )(tokens, grad_out, error[0], q_start.T)
    return (p_factor.T, q_factor.T)


def solution(mesh):
    in_specs = (P("dp", "tensor"), P("dp", "tensor"), P("dp", None, "tensor"), P("tensor", None))
    out_specs = (P(), P("tensor", None))
    return jax.shard_map(
        on_device, mesh=mesh, in_specs=in_specs, out_specs=out_specs, check_vma=False
    )
```

time: 65 us -> 58.5 us (0.900)
  Pallas kernels: 59.3 us -> 54.4 us
  local copies, waits for them, and re-layouts: 4.89 us -> 3.36 us
    pallas_call x1, Pallas kernels: 59.3 us -> 54.4 us  [on_device(): pl.pallas_call(kernel, out_shape=(jax.ShapeDtypeStruct((rank, width), F32...]
    unnamed x8 -> x2, local copies, waits for them, and re-layouts: 4.89 us -> 3.36 us
where the time goes in v2:
time: 58.5 us; the launch traced here: 58.4 us
  Pallas kernels  54.4 us (93%)
  local copies, waits for them, and re-layouts  3.36 us (6%)
  between operations  0.64 us (1%)
    pallas_call x1, Pallas kernels, on_device(): pl.pallas_call(kernel, out_shape=(jax.ShapeDtypeStruct((rank, width), F32...  54.4 us
    unnamed x2, local copies, waits for them, and re-layouts  3.36 us

profile of v2, /device:TPU:1, one launch (start us, length us, event | category | flops | bytes accessed | tf_op | source)
XLA Modules:
  0.0 58.4 jit_solution(4782462220360053792)
XLA Ops:
  0.6 54.4 %shard_map.59 = (f32[32,2560]{1,0:T(8,128)}, f32[32,1792]{1,0:T(8,128)}) custom-call(bf16[512,640]{1,0:T(8,128)(2,1)} %tokens_hbm.1, bf16[512,1792]{1,0:T(8,128)(2,1)} %outs_hbm.1, bf16[2560,1792]{1,0:T(8,128)(2,1)} %bitcast.4, bf16[32,1792]{1,0:T(8,128)(2,1)} %bitcast.7), custom_call_target="tpu_custom_call" | custom-call | tf_op jit(solution)/shard_map/pallas_call | solution.py:243
  55.0 1.7 %copy.8 = f32[2560,32]{0,1:T(8,128)} copy(f32[2560,32]{0,1:T(8,128)} %bitcast.5) | data formatting | bytes 655360
  56.8 1.6 %copy.9 = f32[1792,32]{0,1:T(8,128)} copy(f32[1792,32]{0,1:T(8,128)} %bitcast.6) | data formatting | bytes 458752

commit v3 on v2

--- a/solution.py
+++ b/solution.py
@@ -47,9 +47,9 @@
 
 
 def kernel(
-    tokens_hbm, outs_hbm, error_hbm, q_hbm, p_ref, q_ref,
+    tokens_hbm, outs_hbm, error_hbm, q_hbm, p_ref, scaled_ref, u_all,
     tokens, outs, error, q, gq, gq_in, p_mine, p_core, p_xy, own, own_in, p_z, p_all,
-    v, v_in, u, u_in, u_z, u_all,
+    v, v_in, u, u_in, u_z,
     load_sem, gq_sem, core_sem, xy_sem, own_sem, z_sem, near_sem, all_sem, sib_sem, v_sem, u_sem, uz_sem, uall_sem,
 ):
     dp, x = lax.axis_index("dp"), lax.axis_index("tensor")
@@ -78,14 +78,6 @@
         copy.start()
         return copy
 
-    q_load = load(q_hbm, q, 0)
-    outs_load = load(outs_hbm, outs, 1)
-    error_load = {}
-    for dx in FAR_FIRST + (0,):
-        at = pl.ds(pl.multiple_of((x + dx) % NX * block, block), block)
-        error_load[dx] = load(error_hbm.at[at], error.at[dx], 3 + dx)
-    tokens_load = load(tokens_hbm, tokens, 2)
-
     plane = [(dx, dy) for dx in FAR_FIRST for dy in (2, 1, 3, 0)]
     beside = [(dy, dc) for dy in (2, 1, 3, 0) for dc in range(NC) if dy or dc]
     along = (4, 3, 5, 2, 6, 1, 7)
@@ -95,11 +87,23 @@
     for friend in friends:
         pl.semaphore_signal(barrier, inc=1, device_id=friend, device_id_type=MESH)
 
+    q_load = load(q_hbm, q, 0)
+    part = outs.shape[0] // 2
+    outs_load = [load(outs_hbm.at[pl.ds(h * part, part)], outs.at[pl.ds(h * part, part)], 3 + NX + h) for h in range(2)]
+    error_load = {}
+    for dx in FAR_FIRST + (0,):
+        at = pl.ds(pl.multiple_of((x + dx) % NX * block, block), block)
+        error_load[dx] = load(error_hbm.at[at], error.at[dx], 3 + dx)
+    tokens_load = load(tokens_hbm, tokens, 2)
+
     q_load.wait()
-    outs_load.wait()
-    gq[...] = mm(q[...], outs[...], NT)
+    for h in range(2):
+        outs_load[h].wait()
+        gq[h] = mm(q[...], outs[h * part : (h + 1) * part, :], NT)
     pl.semaphore_wait(barrier, len(friends))
-    gq_copies = [push(gq, gq_in.at[dx - 1], gq_sem, dx - 1, device(dx)) for dx in FAR_FIRST]
+    gq_copies = [
+        [push(gq.at[h], gq_in.at[dx - 1, h], gq_sem, 2 * dx - 2 + h, device(dx)) for dx in FAR_FIRST] for h in range(2)
+    ]
 
     def piece(ref, yy):
         rows = pl.ds(pl.multiple_of(yy // 2 * 8, 8), 8)
@@ -128,10 +132,11 @@
     copies += pass_on(*before)
 
     tokens_load.wait()
-    for copy in gq_copies:
-        copy.wait_recv()
-    total = gq[...] + gq_in[0] + gq_in[1] + gq_in[2]
-    product = product + folded(mm(two_part(total), tokens[...], NN))
+    for h, arriving in enumerate(gq_copies):
+        for copy in arriving:
+            copy.wait_recv()
+        total = two_part(gq[h] + gq_in[0, h] + gq_in[1, h] + gq_in[2, h])
+        product = product + folded(mm(total, tokens[h * part : (h + 1) * part, :], NN))
     own[0] = product[:half]
     own[1] = product[half:]
     for dy, dc in beside:
@@ -173,8 +178,10 @@
     for copy in near:
         copy.wait_recv()
     parts = two_part(features(x))
-    v[...] = folded(mm(parts, tokens[...], NT))
-    v_copies = [push(v, v_in.at[dx - 1], v_sem, dx - 1, device(dx)) for dx in FAR_FIRST]
+    v_copies = []
+    for h in range(2):
+        v[h] = folded(mm(parts, tokens[h * part : (h + 1) * part, :], NT))
+        v_copies.append([push(v.at[h], v_in.at[dx - 1, h], v_sem, 2 * dx - 2 + h, device(dx)) for dx in FAR_FIRST])
     result = folded(mm(parts, error[0], NN))
     forward = {}
     for dx in NEAR_FIRST:
@@ -186,10 +193,11 @@
         forward[dx].wait_recv()
         parts = two_part(features((x + NX - dx) % NX))
         result = result + folded(mm(parts, error[NX - dx], NN))
-    for copy in v_copies:
-        copy.wait_recv()
-    total = two_part(v[...] + v_in[0] + v_in[1] + v_in[2])
-    result = result + folded(mm(total, outs[...], NN))
+    for h, copies in enumerate(v_copies):
+        for copy in copies:
+            copy.wait_recv()
+        total = two_part(v[h] + v_in[0, h] + v_in[1, h] + v_in[2, h])
+        result = result + folded(mm(total, outs[h * part : (h + 1) * part, :], NN))
 
     u[0] = result[:half]
     u[1] = result[half:]
@@ -218,6 +226,7 @@
     inverse = inverse_factor(gram)
     p_ref[...] = mm(inverse * math.sqrt(width), p_sum, NN, lax.Precision.HIGHEST)
 
+    scaled_ref[...] = inverse * (1.0 / (NC * NZ * NY * math.sqrt(width)))
     for copy in copies:
         copy.wait_recv()
     total = u_z[0]
@@ -228,33 +237,46 @@
     copies = [push(slot, slot, uall_sem, 2 * dy + dc - 1, device(dy=dy, dc=dc)) for dy, dc in beside]
     for copy in copies:
         copy.wait_recv()
-    scaled = inverse * (1.0 / (NC * NZ * NY * math.sqrt(width)))
+    for copy in sends:
+        copy.wait_send()
+
+
+def finish(p_ref, scaled_ref, u_all, p_hbm, q_hbm, q, sems):
+    p_copy = pltpu.make_async_copy(p_ref, p_hbm, sems.at[0])
+    p_copy.start()
+    long = u_all.shape[-1]
+    copies = []
     for side in range(2):
         total = jnp.concatenate([u_all[0, side], u_all[0, 2 + side], u_all[1, side], u_all[1, 2 + side]], axis=0)
-        q_ref[:, side * long : (side + 1) * long] = mm(scaled, total, NN, lax.Precision.HIGHEST)
-    for copy in sends:
-        copy.wait_send()
+        at = pl.ds(side * long, long)
+        q[:, at] = mm(scaled_ref[...], total, NN, lax.Precision.HIGHEST)
+        copies.append(pltpu.make_async_copy(q.at[:, at], q_hbm.at[:, at], sems.at[1 + side]))
+        copies[-1].start()
+    p_copy.wait()
+    for copy in copies:
+        copy.wait()
 
 
 def on_device(tokens, grad_out, error, q_start):
     width, hidden = error.shape[1:]
     rank, count, own_width = q_start.shape[1], tokens.shape[0], tokens.shape[1]
     vmem, dma = pltpu.VMEM, pltpu.SemaphoreType.DMA
-    p_factor, q_factor = pl.pallas_call(
+    p_factor, scaled, total = pl.pallas_call(
         kernel,
         out_shape=(
             jax.ShapeDtypeStruct((rank, width), F32),
-            jax.ShapeDtypeStruct((rank, hidden), F32),
+            jax.ShapeDtypeStruct((rank, rank), F32),
+            jax.ShapeDtypeStruct((NC, NY, 8, hidden // 2), F32),
         ),
         in_specs=[pl.BlockSpec(memory_space=pl.ANY)] * 4,
-        out_specs=(pl.BlockSpec(memory_space=pltpu.VMEM),) * 2,
+        out_specs=(pl.BlockSpec(memory_space=pltpu.VMEM),) * 3,
         scratch_shapes=[
             vmem((count, own_width), BF16),
             vmem((count, hidden), BF16),
             vmem((NX, own_width, hidden), BF16),
             vmem((rank, hidden), BF16),
-            vmem((rank, count), F32),
-            vmem((NX - 1, rank, count), F32),
+            vmem((2, rank, count // 2), F32),
+            vmem((NX - 1, 2, rank, count // 2), F32),
             vmem((NX - 1, NC, rank // 2, own_width), F32),
             vmem((NX - 1, rank // 2, own_width), F32),
             vmem(((NX - 1) * NY, 8, 384), F32),
@@ -262,14 +284,13 @@
             vmem((NC * NY - 1, 8, 384), F32),
             vmem((NZ, 8, 384), F32),
             vmem((NX, NC, NY, 8, 384), F32),
-            vmem((rank, count), F32),
-            vmem((NX - 1, rank, count), F32),
+            vmem((2, rank, count // 2), F32),
+            vmem((NX - 1, 2, rank, count // 2), F32),
             vmem((NC, rank // 2, hidden), F32),
             vmem((NC * NY - 1, 8, hidden // 2), F32),
             vmem((NZ, 8, hidden // 2), F32),
-            vmem((NC, NY, 8, hidden // 2), F32),
-            dma((3 + NX,)),
-            dma((2, NX - 1)),
+            dma((5 + NX,)),
+            dma((2, 2 * NX - 2)),
             dma((2, NX - 1)),
             dma((2, (NX - 1) * NY)),
             dma((2, NC * NY - 1)),
@@ -277,15 +298,26 @@
             dma((2, NC * NY - 1)),
             dma((2, (NX - 1) * NY)),
             dma((2, NX - 1)),
-            dma((2, NX - 1)),
+            dma((2, 2 * NX - 2)),
             dma((2, NC * NY - 1)),
             dma((2, NZ - 1)),
             dma((2, NC * NY - 1)),
         ],
         compiler_params=pltpu.CompilerParams(
-            collective_id=0, has_side_effects=True, vmem_limit_bytes=60 << 20
+            collective_id=0, has_side_effects=True, vmem_limit_bytes=53 << 20
         ),
     )(tokens, grad_out, error[0], q_start.T)
+    p_factor, q_factor = pl.pallas_call(
+        finish,
+        out_shape=(
+            jax.ShapeDtypeStruct((rank, width), F32),
+            jax.ShapeDtypeStruct((rank, hidden), F32),
+        ),
+        in_specs=[pl.BlockSpec(memory_space=pltpu.VMEM)] * 3,
+        out_specs=(pl.BlockSpec(memory_space=pl.ANY),) * 2,
+        scratch_shapes=[vmem((rank, hidden), F32), dma((3,))],
+        compiler_params=pltpu.CompilerParams(vmem_limit_bytes=53 << 20),
+    )(p_factor, scaled, total)
     return (p_factor.T, q_factor.T)
 
 

time: 58.5 us -> 54.6 us (0.933)
  local copies, waits for them, and re-layouts: 3.36 us -> 0.89 us
  Pallas kernels: 54.4 us -> 52.9 us
    pallas_call x1, Pallas kernels: 54.4 us -> 51.9 us  [on_device(): pl.pallas_call(kernel, out_shape=(jax.ShapeDtypeStruct((rank, width), F32...]
    unnamed x2, local copies, waits for them, and re-layouts: 3.36 us -> 0.89 us
    pallas_call x0 -> x1, Pallas kernels: none -> 1.02 us  [on_device(): pl.pallas_call(finish, out_shape=(jax.ShapeDtypeStruct((rank, width), F32...]
where the time goes in v3:
time: 54.6 us; the launch traced here: 54.5 us
  Pallas kernels  52.9 us (97%)
  local copies, waits for them, and re-layouts  0.89 us (2%)
  between operations  0.65 us (1%)
    pallas_call x1, Pallas kernels, on_device(): pl.pallas_call(kernel, out_shape=(jax.ShapeDtypeStruct((rank, width), F32...  51.9 us

profile of v3, /device:TPU:1, one launch (start us, length us, event | category | flops | bytes accessed | tf_op | source)
XLA Modules:
  0.0 54.5 jit_solution(10014753282919523714)
XLA Ops:
  0.6 0.0 copy-start
  0.6 0.9 %copy-done = bf16[1792,32]{0,1:T(8,128)(2,1)S(1)} copy-done((bf16[1792,32]{0,1:T(8,128)(2,1)S(1)}, bf16[1792,32]{0,1:T(8,128)(2,1)}, u32[]{:S(2)}) %copy-start) | copy-done | bytes 114712
  1.5 51.9 %shard_map.59 = (f32[32,2560]{1,0:T(8,128)S(1)}, f32[32,32]{1,0:T(8,128)S(1)}, f32[2,4,8,896]{3,2,1,0:T(8,128)S(1)}) custom-call(bf16[512,640]{1,0:T(8,128)(2,1)} %tokens_hbm.1, bf16[512,1792]{1,0:T(8,128)(2,1)} %outs_hbm.1, bf16[2560,1792]{1,0:T(8,128)(2,1)} %bitcast.5, bf16[32,1792]{1,0:T(8,128)(2,1)S(1)} %bitcast.4), custom_call_target="tpu_custom_call" | custom-call | tf_op jit(solution)/shard_map/pallas_call | solution.py:264
  53.5 1.0 %shard_map.60 = (f32[32,2560]{1,0:T(8,128)}, f32[32,1792]{1,0:T(8,128)}) custom-call(f32[32,2560]{1,0:T(8,128)S(1)} %get-tuple-element.7.p_ref, f32[32,32]{1,0:T(8,128)S(1)} %get-tuple-element.8.scaled_ref, f32[2,4,8,896]{3,2,1,0:T(8,128)S(1)} %get-tuple-element.9.u_all), custom_call_target="tpu_custom_call" | custom-call | tf_op jit(solution)/shard_map/pallas_call | solution.py:310
Async XLA Ops:
  0.6 0.9 %copy-start = (bf16[1792,32]{0,1:T(8,128)(2,1)S(1)}, bf16[1792,32]{0,1:T(8,128)(2,1)}, u32[]{:S(2)}) copy-start(bf16[1792,32]{0,1:T(8,128)(2,1)} %param.7) | copy-start | bytes 344068

commit v4 on v3

--- a/solution.py
+++ b/solution.py
@@ -82,8 +82,9 @@
     beside = [(dy, dc) for dy in (2, 1, 3, 0) for dc in range(NC) if dy or dc]
     along = (4, 3, 5, 2, 6, 1, 7)
     barrier = pltpu.get_barrier_semaphore()
-    friends = [device(dx, dy) for dx, dy in plane] + [device(dy=dy, dc=dc) for dy, dc in beside]
-    friends += [device(dz=d) for d in along]
+    friends = [device(*plane[0]), device(dz=along[0])] + [device(dz=d) for d in along[1:3]]
+    friends += [device(dx, dy) for dx, dy in plane[1:]] + [device(dz=d) for d in along[3:]]
+    friends += [device(dy=dy, dc=dc) for dy, dc in beside]
     for friend in friends:
         pl.semaphore_signal(barrier, inc=1, device_id=friend, device_id_type=MESH)
 
@@ -306,7 +307,7 @@
         compiler_params=pltpu.CompilerParams(
             collective_id=0, has_side_effects=True, vmem_limit_bytes=53 << 20
         ),
-    )(tokens, grad_out, error[0], q_start.T)
+    )(*(pltpu.with_memory_space_constraint(a, pltpu.HBM) for a in (tokens, grad_out, error[0], q_start.T)))
     p_factor, q_factor = pl.pallas_call(
         finish,
         out_shape=(

time: 54.6 us -> 53.7 us (0.984)
  local copies, waits for them, and re-layouts: 0.89 us -> 0 us
    unnamed x2 -> x0, local copies, waits for them, and re-layouts: 0.89 us -> none
where the time goes in v4:
time: 53.7 us; the launch traced here: 53.6 us
  Pallas kernels  53 us (99%)
  between operations  0.64 us (1%)
    pallas_call x1, Pallas kernels, on_device(): pl.pallas_call(kernel, out_shape=(jax.ShapeDtypeStruct((rank, width), F32...  51.9 us

profile of v4, /device:TPU:1, one launch (start us, length us, event | category | flops | bytes accessed | tf_op | source)
XLA Modules:
  0.0 53.6 jit_solution(10170740901258208046)
XLA Ops:
  0.6 51.9 %shard_map.59 = (f32[32,2560]{1,0:T(8,128)S(1)}, f32[32,32]{1,0:T(8,128)S(1)}, f32[2,4,8,896]{3,2,1,0:T(8,128)S(1)}) custom-call(bf16[512,640]{1,0:T(8,128)(2,1)} %tokens_hbm.1, bf16[512,1792]{1,0:T(8,128)(2,1)} %outs_hbm.1, bf16[2560,1792]{1,0:T(8,128)(2,1)} %bitcast.4, bf16[32,1792]{1,0:T(8,128)(2,1)} %bitcast.5), custom_call_target="tpu_custom_call" | custom-call | tf_op jit(solution)/shard_map/pallas_call | solution.py:265
  52.6 1.0 %shard_map.60 = (f32[32,2560]{1,0:T(8,128)}, f32[32,1792]{1,0:T(8,128)}) custom-call(f32[32,2560]{1,0:T(8,128)S(1)} %get-tuple-element.7.p_ref, f32[32,32]{1,0:T(8,128)S(1)} %get-tuple-element.8.scaled_ref, f32[2,4,8,896]{3,2,1,0:T(8,128)S(1)} %get-tuple-element.9.u_all), custom_call_target="tpu_custom_call" | custom-call | tf_op jit(solution)/shard_map/pallas_call | solution.py:311

commit v5 on v4

--- a/solution.py
+++ b/solution.py
@@ -203,22 +203,31 @@
     u[0] = result[:half]
     u[1] = result[half:]
 
-    def quarter(dy, dc):
+    spans = [pl.ds(0, 512), pl.ds(512, long - 512)]
+
+    def quarter(dy, dc, k):
         to = (y + dy) % NY
         rows = pl.ds(pl.multiple_of(to // 2 * 8, 8), 8)
-        return u.at[(core + dc) % NC, rows, pl.ds(pl.multiple_of(to % 2 * long, 128), long)]
+        at = pl.multiple_of(to % 2 * long + spans[k].start, 128)
+        return u.at[(core + dc) % NC, rows, pl.ds(at, spans[k].size)]
 
     copies = [
-        push(quarter(dy, dc), u_in.at[2 * dy + dc - 1], u_sem, 2 * dy + dc - 1, device(dy=dy, dc=dc))
-        for dy, dc in beside
+        [
+            push(quarter(dy, dc, k), u_in.at[2 * dy + dc - 1, :, span], u_sem, 7 * k + 2 * dy + dc - 1, device(dy=dy, dc=dc))
+            for dy, dc in beside
+        ]
+        for k, span in enumerate(spans)
     ]
-    total = quarter(0, 0)[...]
-    for copy in copies:
-        copy.wait_recv()
-    for i in range(7):
-        total = total + u_in[i]
-    u_z[z] = total
-    copies = [push(u_z.at[z], u_z.at[z], uz_sem, d - 1, device(dz=d)) for d in along]
+    z_copies = []
+    for k, span in enumerate(spans):
+        total = quarter(0, 0, k)[...]
+        for copy in copies[k]:
+            copy.wait_recv()
+        for i in range(7):
+            total = total + u_in[i, :, span]
+        u_z[z, :, span] = total
+        slot = u_z.at[z, :, span]
+        z_copies.append([push(slot, slot, uz_sem, 7 * k + d - 1, device(dz=d)) for d in along])
 
     for at in range(NX):
         p_ref[:, at * block : (at + 1) * block] = features(at)
@@ -228,14 +237,16 @@
     p_ref[...] = mm(inverse * math.sqrt(width), p_sum, NN, lax.Precision.HIGHEST)
 
     scaled_ref[...] = inverse * (1.0 / (NC * NZ * NY * math.sqrt(width)))
-    for copy in copies:
-        copy.wait_recv()
-    total = u_z[0]
-    for d in range(1, NZ):
-        total = total + u_z[d]
-    slot = u_all.at[core, y]
-    slot[...] = total
-    copies = [push(slot, slot, uall_sem, 2 * dy + dc - 1, device(dy=dy, dc=dc)) for dy, dc in beside]
+    copies = []
+    for k, span in enumerate(spans):
+        for copy in z_copies[k]:
+            copy.wait_recv()
+        total = u_z[0, :, span]
+        for d in range(1, NZ):
+            total = total + u_z[d, :, span]
+        u_all[core, y, :, span] = total
+        slot = u_all.at[core, y, :, span]
+        copies += [push(slot, slot, uall_sem, 7 * k + 2 * dy + dc - 1, device(dy=dy, dc=dc)) for dy, dc in beside]
     for copy in copies:
         copy.wait_recv()
     for copy in sends:
@@ -300,9 +311,9 @@
             dma((2, (NX - 1) * NY)),
             dma((2, NX - 1)),
             dma((2, 2 * NX - 2)),
-            dma((2, NC * NY - 1)),
-            dma((2, NZ - 1)),
-            dma((2, NC * NY - 1)),
+            dma((2, 14)),
+            dma((2, 14)),
+            dma((2, 14)),
         ],
         compiler_params=pltpu.CompilerParams(
             collective_id=0, has_side_effects=True, vmem_limit_bytes=53 << 20

time: 53.7 us -> 53.5 us (level)
  no operation moved by 1% of the time
where the time goes in v5:
time: 53.5 us; the launch traced here: 53.4 us
  Pallas kernels  52.8 us (99%)
  between operations  0.64 us (1%)
    pallas_call x1, Pallas kernels, on_device(): pl.pallas_call(kernel, out_shape=(jax.ShapeDtypeStruct((rank, width), F32...  51.8 us

profile of v5, /device:TPU:1, one launch (start us, length us, event | category | flops | bytes accessed | tf_op | source)
XLA Modules:
  0.0 53.4 jit_solution(8751341132013269012)
XLA Ops:
  0.6 51.8 %shard_map.59 = (f32[32,2560]{1,0:T(8,128)S(1)}, f32[32,32]{1,0:T(8,128)S(1)}, f32[2,4,8,896]{3,2,1,0:T(8,128)S(1)}) custom-call(bf16[512,640]{1,0:T(8,128)(2,1)} %tokens_hbm.1, bf16[512,1792]{1,0:T(8,128)(2,1)} %outs_hbm.1, bf16[2560,1792]{1,0:T(8,128)(2,1)} %bitcast.4, bf16[32,1792]{1,0:T(8,128)(2,1)} %bitcast.5), custom_call_target="tpu_custom_call" | custom-call | tf_op jit(solution)/shard_map/pallas_call | solution.py:276
  52.4 1.0 %shard_map.60 = (f32[32,2560]{1,0:T(8,128)}, f32[32,1792]{1,0:T(8,128)}) custom-call(f32[32,2560]{1,0:T(8,128)S(1)} %get-tuple-element.7.p_ref, f32[32,32]{1,0:T(8,128)S(1)} %get-tuple-element.8.scaled_ref, f32[2,4,8,896]{3,2,1,0:T(8,128)S(1)} %get-tuple-element.9.u_all), custom_call_target="tpu_custom_call" | custom-call | tf_op jit(solution)/shard_map/pallas_call | solution.py:322
